TPU v7x, 32 devices: a whole 2x2x4 slice. The times are simulated.
32 devices in a mesh: axial: 8 (over y, x, core), trans: 4 (over z).
Axes of the slice: x: 2, y: 2, z: 4, core: 2. Of those that a mesh axis runs over, the one named last changes fastest.
Arguments:
- concentration: float32 [128, 32, 256], P('axial', 'trans'), may hold values from -4 to 4
- pore_mask: int32 [128, 32, 256], P('axial', 'trans'), may hold values 0 or 1
- velocity: float32 [128, 32, 256], P('axial', 'trans'), may hold values from 20 to 80
Outputs:
- new_concentration: float32 [128, 32, 256], P('axial', 'trans')
All inputs are finite; a program needn't handle non-finite values. No bound on the sum of `pore_mask` on one device may be relied on, other than what follows from the above.
Results may differ from a plain program's by a relative error of at most 0.00028.
Values sent between devices are 32-bit elements; how exact they have to be, the bound alone decides.
A program may use at most 64 MiB of HBM per device.

v0:
```python
import jax
import jax.numpy as jnp
from jax import lax
from jax.sharding import PartitionSpec as P

axial_number = 800.0
trans_number = 0.5


def padded(cells, sides, width):
    for axis, dim in sides:
        count = lax.axis_size(axis)
        ends = count - 1
        head = lax.slice_in_dim(cells, 0, width, axis=dim)
        tail = lax.slice_in_dim(cells, cells.shape[dim] - width, cells.shape[dim], axis=dim)
        cells = jnp.concatenate(
            [
                lax.ppermute(tail, axis, [(i, (i + 1) % count) for i in range(ends)]),
                cells,
                lax.ppermute(head, axis, [((i + 1) % count, i) for i in range(ends)]),
            ],
            axis=dim,
        )
    return cells


def plane_term(field_pad, phi_pad, field_data, axis_dim):
    cells = field_data.shape[axis_dim]
    face_share = 0.5 * (
        lax.slice_in_dim(phi_pad, 0, cells + 1, axis=axis_dim)
        + lax.slice_in_dim(phi_pad, 1, cells + 2, axis=axis_dim)
    )
    upper_part = lax.slice_in_dim(face_share, 1, cells + 1, axis=axis_dim) * (
        lax.slice_in_dim(field_pad, 2, cells + 2, axis=axis_dim) - field_data
    )
    lower_part = lax.slice_in_dim(face_share, 0, cells, axis=axis_dim) * (
        lax.slice_in_dim(field_pad, 0, cells, axis=axis_dim) - field_data
    )
    return upper_part + lower_part


def eliminate(below_coef, main_coef, above_coef, rhs):
    cell_count = main_coef.shape[0]
    first_src = jnp.concatenate([-below_coef[1:2], jnp.zeros_like(main_coef[2 : cell_count - 1])])
    last_src = jnp.concatenate(
        [
            jnp.zeros_like(main_coef[1 : cell_count - 2]),
            -above_coef[cell_count - 2 : cell_count - 1],
        ]
    )
    sources = jnp.stack([first_src, last_src, rhs[1 : cell_count - 1]], axis=1)

    def forward(running, row_data):
        ratios, partials = running
        below_row, main_row, above_row, source_row = row_data
        pivot_value = main_row - below_row * ratios
        new_ratios = above_row / pivot_value
        new_partials = (source_row - below_row[None] * partials) / pivot_value[None]
        return ((new_ratios, new_partials), (new_ratios, new_partials))

    start_state = (jnp.zeros_like(main_coef[0]), jnp.zeros_like(sources[0]))
    inputs_inner = (
        below_coef[1 : cell_count - 1],
        main_coef[1 : cell_count - 1],
        above_coef[1 : cell_count - 1],
        sources,
    )
    _, (ratio_rows, partial_rows) = lax.scan(forward, start_state, inputs_inner)

    def backward(next_value, row_data):
        ratios, partials = row_data
        now_value = partials - ratios[None] * next_value
        return (now_value, now_value)

    _, interior = lax.scan(
        backward, jnp.zeros_like(partial_rows[0]), (ratio_rows, partial_rows), reverse=True
    )
    last_cell = cell_count - 1
    first_lower = below_coef[0]
    first_main = main_coef[0] + above_coef[0] * interior[0, 0]
    first_upper = above_coef[0] * interior[0, 1]
    first_rhs = rhs[0] - above_coef[0] * interior[0, 2]
    last_lower = below_coef[last_cell] * interior[-1, 0]
    last_main = main_coef[last_cell] + below_coef[last_cell] * interior[-1, 1]
    last_upper = above_coef[last_cell]
    last_rhs = rhs[last_cell] - below_coef[last_cell] * interior[-1, 2]
    reduced = jnp.stack(
        [
            jnp.stack([first_lower, last_lower]),
            jnp.stack([first_main, last_main]),
            jnp.stack([first_upper, last_upper]),
            jnp.stack([first_rhs, last_rhs]),
        ]
    )
    return (reduced, interior)


def assemble(first_cell, last_cell, interior):
    inner_cells = (
        interior[:, 0] * first_cell[None] + interior[:, 1] * last_cell[None] + interior[:, 2]
    )
    return jnp.concatenate([first_cell[None], inner_cells, last_cell[None]])


def reduce_cyclic(lower_part, main_part, upper_part, right_part):
    row_count = lower_part.shape[0]
    for stride_level in range(row_count.bit_length() - 1):
        stride = 2**stride_level

        def from_lower(values, fill_value):
            return jnp.concatenate(
                [jnp.full_like(values[:stride], fill_value), values[: row_count - stride]]
            )

        def from_upper(values, fill_value):
            return jnp.concatenate([values[stride:], jnp.full_like(values[:stride], fill_value)])

        factor_low = lower_part / from_lower(main_part, 1.0)
        factor_high = upper_part / from_upper(main_part, 1.0)
        new_lower = -factor_low * from_lower(lower_part, 0.0)
        new_main = (
            main_part
            - factor_low * from_lower(upper_part, 0.0)
            - factor_high * from_upper(lower_part, 0.0)
        )
        new_upper = -factor_high * from_upper(upper_part, 0.0)
        new_right = (
            right_part
            - factor_low * from_lower(right_part, 0.0)
            - factor_high * from_upper(right_part, 0.0)
        )
        lower_part, main_part, upper_part, right_part = (new_lower, new_main, new_upper, new_right)
    return right_part / main_part


def body(concentration, pore_mask, velocity):
    porosity = 0.1 + 0.9 * pore_mask.astype(jnp.float32)
    axial_ext = padded(jnp.stack([concentration, porosity, velocity]), (("axial", 1),), 1)
    conc_ext = axial_ext[0]
    phi_ext = axial_ext[1]
    vel_ext = axial_ext[2]
    face_share = 0.5 * (phi_ext[:-1] + phi_ext[1:])
    advect = 0.5 * (vel_ext[:-1] + vel_ext[1:]) * face_share
    spread = axial_number * face_share
    lower_coef = advect[:-1] + spread[:-1]
    upper_coef = spread[1:]
    center = spread[:-1] + spread[1:] + advect[1:]
    axial_term = lower_coef * conc_ext[:-2] - center * concentration + upper_coef * conc_ext[2:]
    plane_ext = padded(jnp.stack([concentration, porosity]), (("trans", 2),), 1)
    transverse = plane_term(plane_ext[0], plane_ext[1], concentration, 1)
    z_widths = ((0, 0), (0, 0), (1, 1))
    transverse = transverse + plane_term(
        jnp.pad(concentration, z_widths), jnp.pad(porosity, z_widths), concentration, 2
    )
    rhs = concentration + axial_term + trans_number * transverse
    below_coef = -lower_coef
    main_coef = 1.0 + center
    above_coef = -upper_coef
    device_index = lax.axis_index("axial")
    reduced, interior = eliminate(below_coef, main_coef, above_coef, rhs)
    gathered = lax.all_gather(reduced, "axial", axis=1, tiled=True)
    all_ends = reduce_cyclic(gathered[0], gathered[1], gathered[2], gathered[3])
    end_values = lax.dynamic_slice_in_dim(all_ends, 2 * device_index, 2, 0)
    return assemble(end_values[0], end_values[1], interior)


def solution(mesh):
    in_specs = (P("axial", "trans", None), P("axial", "trans", None), P("axial", "trans", None))
    out_specs = P("axial", "trans", None)
    return jax.shard_map(body, mesh=mesh, in_specs=in_specs, out_specs=out_specs, check_vma=False)
```

profile of v0, /device:TPU:0, one launch (start us, length us, event | category | flops | bytes accessed | tf_op | source)
XLA Modules:
  0.0 33.0 jit_solution(11848905922522627214)
XLA Ops:
  0.0 0.0 copy-start
  0.0 0.0 copy-start.1
  0.0 1.0 %fusion.47 = (f32[1,16,8,256]{3,2,1,0:T(8,128)S(1)}, f32[16,8,256]{2,1,0:T(8,128)S(1)}) fusion(s32[16,8,256]{2,1,0:T(8,128)} %param.8), kind=kLoop, calls=%fused_computation.145 | loop fusion | flops 98304 | bytes 393216 | tf_op jit(solution)/shard_map/stack | solution.py:138
  1.0 0.0 copy-done
  1.0 0.0 copy-done.1
  1.0 2.3 %collective-permute-start = (f32[3,1,8,256]{3,2,1,0:T(8,128)S(1)}, f32[3,1,8,256]{3,2,1,0:T(8,128)S(1)}, u32[]{:S(2)}, u32[]{:S(2)}) collective-permute-start(f32[3,1,8,256]{3,2,1,0:T(8,128)S(1)} %get-tuple-element.278), channel_id=1, source_target_pairs={{0,4},{4,8},{8,12},{12,16},{16,20},{20,24},{24,28},{1,5},{5,9},{9,... | collective-permute-start | bytes 73736 | tf_op jit(solution)/shard_map/ppermute | solution.py:18
  3.4 1.3 %collective-permute-start.1 = (f32[3,1,8,256]{3,2,1,0:T(8,128)S(1)}, f32[3,1,8,256]{3,2,1,0:T(8,128)S(1)}, u32[]{:S(2)}, u32[]{:S(2)}) collective-permute-start(f32[3,1,8,256]{3,2,1,0:T(8,128)S(1)} %get-tuple-element.279), channel_id=1, source_target_pairs={{4,0},{8,4},{12,8},{16,12},{20,16},{24,20},{28,24},{5,1},{9,5},{13... | collective-permute-start | bytes 73736 | tf_op jit(solution)/shard_map/ppermute | solution.py:20
  4.7 4.3 %collective-permute-start.2 = (f32[2,16,1,256]{3,2,1,0:T(1,128)S(1)}, f32[2,16,1,256]{3,2,1,0:T(1,128)S(1)}, u32[]{:S(2)}, u32[]{:S(2)}) collective-permute-start(f32[2,16,1,256]{3,2,1,0:T(1,128)S(1)} %get-tuple-element.282), channel_id=1, source_target_pairs={{0,1},{1,2},{2,3},{4,5},{5,6},{6,7},{8,9},{9,10},{10,11},{12,13},{... | collective-permute-start | bytes 98312 | tf_op jit(solution)/shard_map/ppermute | solution.py:18
  9.1 1.3 %collective-permute-start.3 = (f32[2,16,1,256]{3,2,1,0:T(1,128)S(1)}, f32[2,16,1,256]{3,2,1,0:T(1,128)S(1)}, u32[]{:S(2)}, u32[]{:S(2)}) collective-permute-start(f32[2,16,1,256]{3,2,1,0:T(1,128)S(1)} %get-tuple-element.283), channel_id=1, source_target_pairs={{1,0},{2,1},{3,2},{5,4},{6,5},{7,6},{9,8},{10,9},{11,10},{13,12},{... | collective-permute-start | bytes 98312 | tf_op jit(solution)/shard_map/ppermute | solution.py:20
  10.4 0.1 fusion.3
  10.5 0.0 collective-permute-done
  10.5 0.0 collective-permute-done.1
  10.5 0.1 maximum_maximum_fusion
  10.8 0.0 copy-start.2
  10.8 0.6 %copy-done.2 = f32[16,8,256]{2,1,0:T(8,128)} copy-done((f32[16,8,256]{2,1,0:T(8,128)}, f32[16,8,256]{2,1,0:T(8,128)S(1)}, u32[]{:S(2)}) %copy-start.2) | copy-done | bytes 131096
  11.4 0.0 collective-permute-done.2
  11.4 3.4 %collective-permute-done.3 = f32[2,16,1,256]{3,2,1,0:T(1,128)S(1)} collective-permute-done((f32[2,16,1,256]{3,2,1,0:T(1,128)S(1)}, f32[2,16,1,256]{3,2,1,0:T(1,128)S(1)}, u32[]{:S(2)}, u32[]{:S(2)}) %collective-permute-start.3) | collective-permute-done | bytes 32800 | tf_op jit(solution)/shard_map/ppermute | solution.py:20
  14.9 0.1 pad_maximum_fusion
  15.1 0.2 fusion.11
  15.3 0.0 slice-start
  15.4 0.9 %slice-done = f32[14,8,256]{2,1,0:T(8,128)S(1)} async-done(((f32[16,8,256]{2,1,0:T(8,128)}), f32[14,8,256]{2,1,0:T(8,128)S(1)}, s32[]{:S(2)}) %slice-start) | async-done | bytes 114712 | tf_op jit(solution)/shard_map/slice | solution.py:64
  16.2 0.9 %while.34 = (s32[]{:T(128)}, f32[8,256]{1,0:T(8,128)S(1)}, f32[3,8,256]{2,1,0:T(8,128)S(1)}, f32[14,8,256]{2,1,0:T(8,128)S(1)}, f32[14,3,8,256]{3,2,1,0:T(8,128)...) while((s32[]{:T(128)}, f32[8,256]{1,0:T(8,128)S(1)}, ...), condition=%wide.region_1.2_spmd.clone, body=%wide.region_0.1_spmd.clone.sunk | while | flops 32771 | bytes 180352 | solution.py:68
  17.1 0.0 copy-start.3
  17.1 0.8 %while.35 = (s32[]{:T(128)}, f32[3,8,256]{2,1,0:T(8,128)S(1)}, f32[14,3,8,256]{3,2,1,0:T(8,128)S(1)}, f32[14,3,8,256]{3,2,1,0:T(8,128)S(1)}, f32[14,8,256]{2,1,0...) while((s32[]{:T(128)}, f32[3,8,256]{2,1,0:T(8,128)S(1)}, f32[14,3,8,256]{3,2,1,0:T(8,128)S(1)}, ...), condition=%wide.region_3.4_spmd.clone, body=%wide.region_2.3_spmd.clone.sunk | while | flops 18436 | bytes 122995 | solution.py:75
  18.0 0.1 copy-done.3
  18.1 13.3 %all_gather.3 = f32[4,16,8,256]{3,2,1,0:T(8,128)S(1)} all-gather(f32[4,2,8,256]{3,2,1,0:T(8,128)S(1)} %pad_maximum_fusion.4), channel_id=1, replica_groups=mesh['axial'=8,'trans'=4] {'axial'}, dimensions={1}, use_global_device_ids=true | all-gather | bytes 589824 | tf_op jit(solution)/shard_map/all_gather | solution.py:161
  31.4 0.1 slice_bitcast_fusion.9
  31.5 0.1 fusion.15
  31.6 0.1 multiply_subtract_fusion.3
  31.8 0.1 multiply_subtract_fusion.2
  31.9 0.1 multiply_subtract_fusion.1
  32.1 0.1 pad_multiply_fusion.1
  32.3 0.7 %pad_maximum_fusion.3 = f32[16,8,256]{2,1,0:T(8,128)} fusion(f32[1,8,256]{2,1,0:T(8,128)S(1)} %get-tuple-element.316, f32[14,8,256]{2,1,0:T(8,128)S(1)} %fusion.29, f32[1,8,256]{2,1,0:T(8,128)S(1)} %get-tuple-element.313), kind=kLoop, calls=%fused_computation.64 | loop fusion | flops 65536 | bytes 262144 | tf_op jit(solution)/shard_map/concatenate | solution.py:102
  (97 shorter events, 1.4 us)
Async XLA Ops:
  0.0 1.0 %copy-start = (f32[16,8,256]{2,1,0:T(8,128)S(1)}, f32[16,8,256]{2,1,0:T(8,128)}, u32[]{:S(2)}) copy-start(f32[16,8,256]{2,1,0:T(8,128)} %param.7) | copy-start | bytes 393220
  0.0 1.0 %copy-start.1 = (f32[16,8,256]{2,1,0:T(8,128)S(1)}, f32[16,8,256]{2,1,0:T(8,128)}, u32[]{:S(2)}) copy-start(f32[16,8,256]{2,1,0:T(8,128)} %param.9) | copy-start | bytes 393220
  1.0 9.5 %collective-permute-start = (f32[3,1,8,256]{3,2,1,0:T(8,128)S(1)}, f32[3,1,8,256]{3,2,1,0:T(8,128)S(1)}, u32[]{:S(2)}, u32[]{:S(2)}) collective-permute-start(f32[3,1,8,256]{3,2,1,0:T(8,128)S(1)} %get-tuple-element.278), channel_id=1, source_target_pairs={{0,4},{4,8},{8,12},{12,16},{16,20},{20,24},{24,28},{1,5},{5,9},{9,... | collective-permute-start | bytes 73736 | tf_op jit(solution)/shard_map/ppermute | solution.py:18
  3.4 7.1 %collective-permute-start.1 = (f32[3,1,8,256]{3,2,1,0:T(8,128)S(1)}, f32[3,1,8,256]{3,2,1,0:T(8,128)S(1)}, u32[]{:S(2)}, u32[]{:S(2)}) collective-permute-start(f32[3,1,8,256]{3,2,1,0:T(8,128)S(1)} %get-tuple-element.279), channel_id=1, source_target_pairs={{4,0},{8,4},{12,8},{16,12},{20,16},{24,20},{28,24},{5,1},{9,5},{13... | collective-permute-start | bytes 73736 | tf_op jit(solution)/shard_map/ppermute | solution.py:20
  4.7 6.7 %collective-permute-start.2 = (f32[2,16,1,256]{3,2,1,0:T(1,128)S(1)}, f32[2,16,1,256]{3,2,1,0:T(1,128)S(1)}, u32[]{:S(2)}, u32[]{:S(2)}) collective-permute-start(f32[2,16,1,256]{3,2,1,0:T(1,128)S(1)} %get-tuple-element.282), channel_id=1, source_target_pairs={{0,1},{1,2},{2,3},{4,5},{5,6},{6,7},{8,9},{9,10},{10,11},{12,13},{... | collective-permute-start | bytes 98312 | tf_op jit(solution)/shard_map/ppermute | solution.py:18
  9.1 5.8 %collective-permute-start.3 = (f32[2,16,1,256]{3,2,1,0:T(1,128)S(1)}, f32[2,16,1,256]{3,2,1,0:T(1,128)S(1)}, u32[]{:S(2)}, u32[]{:S(2)}) collective-permute-start(f32[2,16,1,256]{3,2,1,0:T(1,128)S(1)} %get-tuple-element.283), channel_id=1, source_target_pairs={{1,0},{2,1},{3,2},{5,4},{6,5},{7,6},{9,8},{10,9},{11,10},{13,12},{... | collective-permute-start | bytes 98312 | tf_op jit(solution)/shard_map/ppermute | solution.py:20
  10.8 0.7 %copy-start.2 = (f32[16,8,256]{2,1,0:T(8,128)}, f32[16,8,256]{2,1,0:T(8,128)S(1)}, u32[]{:S(2)}) copy-start(f32[16,8,256]{2,1,0:T(8,128)S(1)} %broadcast_add_fusion) | copy-start | bytes 393220
  15.3 0.9 %slice-start = ((f32[16,8,256]{2,1,0:T(8,128)}), f32[14,8,256]{2,1,0:T(8,128)S(1)}, s32[]{:S(2)}) async-start(f32[16,8,256]{2,1,0:T(8,128)} %copy-done.2), calls=%async_computation | async-start | bytes 229376 | tf_op jit(solution)/shard_map/slice | solution.py:64
  17.1 0.9 %copy-start.3 = (f32[16,8,256]{2,1,0:T(8,128)S(1)}, f32[16,8,256]{2,1,0:T(8,128)}, u32[]{:S(2)}) copy-start(f32[16,8,256]{2,1,0:T(8,128)} %copy-done.2) | copy-start | bytes 393220
where the time goes:
time: 33.2 us; the launch traced here: 33 us
  blocking collectives  13.3 us (40%)
  starting transfers between devices  9.24 us (28%)
  other arithmetic  3.51 us (11%)
  waiting for transfers between devices  3.45 us (10%)
  local copies, waits for them, and re-layouts  2.09 us (6%)
  loops' own time  0.93 us (3%)
  between operations  0.44 us (1%)
    all_gather x1, blocking collectives, body(): gathered = lax.all_gather(reduced, 'axial', axis=1, tiled=True)  13.3 us
    ppermute x2, starting transfers between devices, padded(): lax.ppermute(tail, axis, [(i, (i + 1) % count) for i in range(ends)])  6.66 us
    ppermute x2, waiting for transfers between devices, padded(): lax.ppermute(head, axis, [((i + 1) % count, i) for i in range(ends)])  3.45 us
    ppermute x2, starting transfers between devices, padded(): lax.ppermute(head, axis, [((i + 1) % count, i) for i in range(ends)])  2.58 us
    another operation x1, other arithmetic, body(): jnp.stack([concentration, porosity, velocity])  0.97 us
    slice x2, local copies, waits for them, and re-layouts, eliminate(): main_coef[1:cell_count - 1]  0.86 us
    unnamed x8, local copies, waits for them, and re-layouts  0.75 us
    concatenate x1, other arithmetic, assemble(): return jnp.concatenate([first_cell[None], inner_cells, last_cell[None]])  0.67 us
  transfers between devices with their start and end apart: 4, of which 1 were waited for; matrix products, arithmetic and copies ran while one was open for 1% of the time, Pallas kernels for 0%

commit v1 on v0

--- a/solution.py
+++ b/solution.py
@@ -158,7 +158,26 @@
     above_coef = -upper_coef
     device_index = lax.axis_index("axial")
     reduced, interior = eliminate(below_coef, main_coef, above_coef, rhs)
-    gathered = lax.all_gather(reduced, "axial", axis=1, tiled=True)
+    devices, index, extent = (lax.axis_size("axial"), lax.axis_index("axial"), reduced.shape[1])
+    upward = [(i_2, (i_2 + 1) % devices) for i_2 in range(devices)]
+    backward_2 = [(i_2, (i_2 - 1) % devices) for i_2 in range(devices)]
+    filled = jnp.zeros(
+        (*reduced.shape[:1], devices * extent, *reduced.shape[1 + 1 :]), reduced.dtype
+    )
+    filled = lax.dynamic_update_slice_in_dim(filled, reduced, index * extent, axis=1)
+    from_left = from_right = reduced
+    half = devices // 2
+    for step in range(1, half + 1):
+        from_left = lax.ppermute(from_left, "axial", upward)
+        filled = lax.dynamic_update_slice_in_dim(
+            filled, from_left, (index - step) % devices * extent, axis=1
+        )
+        if step < devices - half:
+            from_right = lax.ppermute(from_right, "axial", backward_2)
+            filled = lax.dynamic_update_slice_in_dim(
+                filled, from_right, (index + step) % devices * extent, axis=1
+            )
+    gathered = filled
     all_ends = reduce_cyclic(gathered[0], gathered[1], gathered[2], gathered[3])
     end_values = lax.dynamic_slice_in_dim(all_ends, 2 * device_index, 2, 0)
     return assemble(end_values[0], end_values[1], interior)

time: 33.2 us -> 41 us (1.23)
  the two profiles are of different devices: /device:TPU:0 before, /device:TPU:20 now
where the time goes in v1:
time: 41 us; the launch traced here: 40.8 us
  starting transfers between devices  20.4 us (50%)
  waiting for transfers between devices  13.2 us (32%)
  other arithmetic  3.51 us (9%)
  local copies, waits for them, and re-layouts  2.19 us (5%)
  loops' own time  0.93 us (2%)
  between operations  0.5 us (1%)
    ppermute x4, waiting for transfers between devices, body(): from_left = lax.ppermute(from_left, 'axial', upward)  10.6 us
    ppermute x3, starting transfers between devices, body(): from_right = lax.ppermute(from_right, 'axial', backward_2)  8.08 us
    ppermute x2, starting transfers between devices, padded(): lax.ppermute(head, axis, [((i + 1) % count, i) for i in range(ends)])  6.9 us
    ppermute x2, starting transfers between devices, padded(): lax.ppermute(tail, axis, [(i, (i + 1) % count) for i in range(ends)])  5.39 us
    ppermute x2, waiting for transfers between devices, padded(): lax.ppermute(head, axis, [((i + 1) % count, i) for i in range(ends)])  2.38 us
    another operation x1, other arithmetic, body(): jnp.stack([concentration, porosity, velocity])  0.97 us
    slice x2, local copies, waits for them, and re-layouts, eliminate(): main_coef[1:cell_count - 1]  0.86 us
  transfers between devices with their start and end apart: 11, of which 6 were waited for; matrix products, arithmetic and copies ran while one was open for 1% of the time, Pallas kernels for 0%

profile of v1, /device:TPU:20, one launch (start us, length us, event | category | flops | bytes accessed | tf_op | source)
XLA Modules:
  0.0 40.8 jit_solution(16910277212396187911)
XLA Ops:
  0.0 0.0 copy-start
  0.0 0.0 copy-start.1
  0.0 1.0 %fusion.47 = (f32[1,16,8,256]{3,2,1,0:T(8,128)S(1)}, f32[16,8,256]{2,1,0:T(8,128)S(1)}) fusion(s32[16,8,256]{2,1,0:T(8,128)} %param.8), kind=kLoop, calls=%fused_computation.153 | loop fusion | flops 98304 | bytes 393216 | tf_op jit(solution)/shard_map/stack | solution.py:138
  1.0 0.0 copy-done
  1.0 0.0 copy-done.1
  1.0 1.9 %collective-permute-start = (f32[3,1,8,256]{3,2,1,0:T(8,128)S(1)}, f32[3,1,8,256]{3,2,1,0:T(8,128)S(1)}, u32[]{:S(2)}, u32[]{:S(2)}) collective-permute-start(f32[3,1,8,256]{3,2,1,0:T(8,128)S(1)} %get-tuple-element.278), channel_id=1, source_target_pairs={{0,4},{4,8},{8,12},{12,16},{16,20},{20,24},{24,28},{1,5},{5,9},{9,... | collective-permute-start | bytes 73736 | tf_op jit(solution)/shard_map/ppermute | solution.py:18
  3.0 4.5 %collective-permute-start.1 = (f32[3,1,8,256]{3,2,1,0:T(8,128)S(1)}, f32[3,1,8,256]{3,2,1,0:T(8,128)S(1)}, u32[]{:S(2)}, u32[]{:S(2)}) collective-permute-start(f32[3,1,8,256]{3,2,1,0:T(8,128)S(1)} %get-tuple-element.279), channel_id=1, source_target_pairs={{4,0},{8,4},{12,8},{16,12},{20,16},{24,20},{28,24},{5,1},{9,5},{13... | collective-permute-start | bytes 73736 | tf_op jit(solution)/shard_map/ppermute | solution.py:20
  7.6 3.5 %collective-permute-start.2 = (f32[2,16,1,256]{3,2,1,0:T(1,128)S(1)}, f32[2,16,1,256]{3,2,1,0:T(1,128)S(1)}, u32[]{:S(2)}, u32[]{:S(2)}) collective-permute-start(f32[2,16,1,256]{3,2,1,0:T(1,128)S(1)} %get-tuple-element.282), channel_id=1, source_target_pairs={{0,1},{1,2},{2,3},{4,5},{5,6},{6,7},{8,9},{9,10},{10,11},{12,13},{... | collective-permute-start | bytes 98312 | tf_op jit(solution)/shard_map/ppermute | solution.py:18
  11.0 2.4 %collective-permute-start.3 = (f32[2,16,1,256]{3,2,1,0:T(1,128)S(1)}, f32[2,16,1,256]{3,2,1,0:T(1,128)S(1)}, u32[]{:S(2)}, u32[]{:S(2)}) collective-permute-start(f32[2,16,1,256]{3,2,1,0:T(1,128)S(1)} %get-tuple-element.283), channel_id=1, source_target_pairs={{1,0},{2,1},{3,2},{5,4},{6,5},{7,6},{9,8},{10,9},{11,10},{13,12},{... | collective-permute-start | bytes 98312 | tf_op jit(solution)/shard_map/ppermute | solution.py:20
  13.4 0.1 fusion.3
  13.6 0.0 collective-permute-done
  13.6 0.0 collective-permute-done.1
  13.6 0.1 maximum_maximum_fusion
  13.8 0.0 copy-start.2
  13.9 0.6 %copy-done.2 = f32[16,8,256]{2,1,0:T(8,128)} copy-done((f32[16,8,256]{2,1,0:T(8,128)}, f32[16,8,256]{2,1,0:T(8,128)S(1)}, u32[]{:S(2)}) %copy-start.2) | copy-done | bytes 131096
  14.5 0.0 collective-permute-done.2
  14.5 2.4 %collective-permute-done.3 = f32[2,16,1,256]{3,2,1,0:T(1,128)S(1)} collective-permute-done((f32[2,16,1,256]{3,2,1,0:T(1,128)S(1)}, f32[2,16,1,256]{3,2,1,0:T(1,128)S(1)}, u32[]{:S(2)}, u32[]{:S(2)}) %collective-permute-start.3) | collective-permute-done | bytes 32800 | tf_op jit(solution)/shard_map/ppermute | solution.py:20
  16.9 0.1 pad_maximum_fusion
  17.0 0.2 fusion.11
  17.3 0.0 slice-start
  17.3 0.9 %slice-done = f32[14,8,256]{2,1,0:T(8,128)S(1)} async-done(((f32[16,8,256]{2,1,0:T(8,128)}), f32[14,8,256]{2,1,0:T(8,128)S(1)}, s32[]{:S(2)}) %slice-start) | async-done | bytes 114712 | tf_op jit(solution)/shard_map/slice | solution.py:64
  18.2 0.9 %while.34 = (s32[]{:T(128)}, f32[8,256]{1,0:T(8,128)S(1)}, f32[3,8,256]{2,1,0:T(8,128)S(1)}, f32[14,8,256]{2,1,0:T(8,128)S(1)}, f32[14,3,8,256]{3,2,1,0:T(8,128)...) while((s32[]{:T(128)}, f32[8,256]{1,0:T(8,128)S(1)}, ...), condition=%wide.region_1.2_spmd.clone, body=%wide.region_0.1_spmd.clone.sunk | while | flops 32771 | bytes 180352 | solution.py:68
  19.1 0.0 copy-start.3
  19.1 0.8 %while.35 = (s32[]{:T(128)}, f32[3,8,256]{2,1,0:T(8,128)S(1)}, f32[14,3,8,256]{3,2,1,0:T(8,128)S(1)}, f32[14,3,8,256]{3,2,1,0:T(8,128)S(1)}, f32[14,8,256]{2,1,0...) while((s32[]{:T(128)}, f32[3,8,256]{2,1,0:T(8,128)S(1)}, f32[14,3,8,256]{3,2,1,0:T(8,128)S(1)}, ...), condition=%wide.region_3.4_spmd.clone, body=%wide.region_2.3_spmd.clone.sunk | while | flops 18436 | bytes 122995 | solution.py:75
  19.9 0.1 copy-done.3
  20.1 0.1 collective-permute-start.4
  20.2 2.6 %collective-permute-start.5 = (f32[4,2,8,256]{3,2,1,0:T(8,128)S(1)}, f32[4,2,8,256]{3,2,1,0:T(8,128)S(1)}, u32[]{:S(2)}, u32[]{:S(2)}) collective-permute-start(f32[4,2,8,256]{3,2,1,0:T(8,128)S(1)} %get-tuple-element.313), channel_id=1, source_target_pairs={{0,28},{4,0},{8,4},{12,8},{16,12},{20,16},{24,20},{28,24},{1,29},{... | collective-permute-start | bytes 196616 | tf_op jit(solution)/shard_map/ppermute | solution.py:176
  22.8 2.6 %collective-permute-done.4 = f32[4,2,8,256]{3,2,1,0:T(8,128)S(1)} collective-permute-done((f32[4,2,8,256]{3,2,1,0:T(8,128)S(1)}, f32[4,2,8,256]{3,2,1,0:T(8,128)S(1)}, u32[]{:S(2)}, u32[]{:S(2)}) %collective-permute-start.4) | collective-permute-done | bytes 65568 | tf_op jit(solution)/shard_map/ppermute | solution.py:171
  25.4 0.0 collective-permute-start.6
  25.4 0.0 collective-permute-done.5
  25.4 2.6 %collective-permute-start.7 = (f32[4,2,8,256]{3,2,1,0:T(8,128)S(1)}, f32[4,2,8,256]{3,2,1,0:T(8,128)S(1)}, u32[]{:S(2)}, u32[]{:S(2)}) collective-permute-start(f32[4,2,8,256]{3,2,1,0:T(8,128)S(1)} %collective-permute-done.5), channel_id=1, source_target_pairs={{0,28},{4,0},{8,4},{12,8},{16,12},{20,16},{24,20},{28,24},{1,29},{... | collective-permute-start | bytes 196616 | tf_op jit(solution)/shard_map/ppermute | solution.py:176
  28.1 1.9 %collective-permute-done.6 = f32[4,2,8,256]{3,2,1,0:T(8,128)S(1)} collective-permute-done((f32[4,2,8,256]{3,2,1,0:T(8,128)S(1)}, f32[4,2,8,256]{3,2,1,0:T(8,128)S(1)}, u32[]{:S(2)}, u32[]{:S(2)}) %collective-permute-start.6) | collective-permute-done | bytes 65568 | tf_op jit(solution)/shard_map/ppermute | solution.py:171
  30.0 0.0 collective-permute-start.8
  30.0 0.0 collective-permute-done.7
  30.1 2.8 %collective-permute-start.9 = (f32[4,2,8,256]{3,2,1,0:T(8,128)S(1)}, f32[4,2,8,256]{3,2,1,0:T(8,128)S(1)}, u32[]{:S(2)}, u32[]{:S(2)}) collective-permute-start(f32[4,2,8,256]{3,2,1,0:T(8,128)S(1)} %collective-permute-done.7), channel_id=1, source_target_pairs={{0,28},{4,0},{8,4},{12,8},{16,12},{20,16},{24,20},{28,24},{1,29},{... | collective-permute-start | bytes 196616 | tf_op jit(solution)/shard_map/ppermute | solution.py:176
  32.9 1.7 %collective-permute-done.8 = f32[4,2,8,256]{3,2,1,0:T(8,128)S(1)} collective-permute-done((f32[4,2,8,256]{3,2,1,0:T(8,128)S(1)}, f32[4,2,8,256]{3,2,1,0:T(8,128)S(1)}, u32[]{:S(2)}, u32[]{:S(2)}) %collective-permute-start.8) | collective-permute-done | bytes 65568 | tf_op jit(solution)/shard_map/ppermute | solution.py:171
  34.6 0.0 collective-permute-start.10
  34.6 0.2 collective-permute-done.9
  34.8 4.4 %collective-permute-done.10 = f32[4,2,8,256]{3,2,1,0:T(8,128)S(1)} collective-permute-done((f32[4,2,8,256]{3,2,1,0:T(8,128)S(1)}, f32[4,2,8,256]{3,2,1,0:T(8,128)S(1)}, u32[]{:S(2)}, u32[]{:S(2)}) %collective-permute-start.10) | collective-permute-done | bytes 65568 | tf_op jit(solution)/shard_map/ppermute | solution.py:171
  39.2 0.1 slice_bitcast_fusion.9
  39.3 0.1 fusion.15
  39.5 0.1 multiply_subtract_fusion.3
  39.6 0.1 multiply_subtract_fusion.2
  39.7 0.1 multiply_subtract_fusion.1
  39.9 0.1 pad_multiply_fusion.1
  40.1 0.7 %pad_maximum_fusion.3 = f32[16,8,256]{2,1,0:T(8,128)} fusion(f32[1,8,256]{2,1,0:T(8,128)S(1)} %get-tuple-element.318, f32[14,8,256]{2,1,0:T(8,128)S(1)} %fusion.29, f32[1,8,256]{2,1,0:T(8,128)S(1)} %get-tuple-element.315), kind=kLoop, calls=%fused_computation.64 | loop fusion | flops 65536 | bytes 262144 | tf_op jit(solution)/shard_map/concatenate | solution.py:102
  (105 shorter events, 1.5 us)
Async XLA Ops:
  0.0 1.0 %copy-start = (f32[16,8,256]{2,1,0:T(8,128)S(1)}, f32[16,8,256]{2,1,0:T(8,128)}, u32[]{:S(2)}) copy-start(f32[16,8,256]{2,1,0:T(8,128)} %param.7) | copy-start | bytes 393220
  0.0 1.0 %copy-start.1 = (f32[16,8,256]{2,1,0:T(8,128)S(1)}, f32[16,8,256]{2,1,0:T(8,128)}, u32[]{:S(2)}) copy-start(f32[16,8,256]{2,1,0:T(8,128)} %param.9) | copy-start | bytes 393220
  1.0 12.5 %collective-permute-start = (f32[3,1,8,256]{3,2,1,0:T(8,128)S(1)}, f32[3,1,8,256]{3,2,1,0:T(8,128)S(1)}, u32[]{:S(2)}, u32[]{:S(2)}) collective-permute-start(f32[3,1,8,256]{3,2,1,0:T(8,128)S(1)} %get-tuple-element.278), channel_id=1, source_target_pairs={{0,4},{4,8},{8,12},{12,16},{16,20},{20,24},{24,28},{1,5},{5,9},{9,... | collective-permute-start | bytes 73736 | tf_op jit(solution)/shard_map/ppermute | solution.py:18
  3.0 10.6 %collective-permute-start.1 = (f32[3,1,8,256]{3,2,1,0:T(8,128)S(1)}, f32[3,1,8,256]{3,2,1,0:T(8,128)S(1)}, u32[]{:S(2)}, u32[]{:S(2)}) collective-permute-start(f32[3,1,8,256]{3,2,1,0:T(8,128)S(1)} %get-tuple-element.279), channel_id=1, source_target_pairs={{4,0},{8,4},{12,8},{16,12},{20,16},{24,20},{28,24},{5,1},{9,5},{13... | collective-permute-start | bytes 73736 | tf_op jit(solution)/shard_map/ppermute | solution.py:20
  7.6 6.9 %collective-permute-start.2 = (f32[2,16,1,256]{3,2,1,0:T(1,128)S(1)}, f32[2,16,1,256]{3,2,1,0:T(1,128)S(1)}, u32[]{:S(2)}, u32[]{:S(2)}) collective-permute-start(f32[2,16,1,256]{3,2,1,0:T(1,128)S(1)} %get-tuple-element.282), channel_id=1, source_target_pairs={{0,1},{1,2},{2,3},{4,5},{5,6},{6,7},{8,9},{9,10},{10,11},{12,13},{... | collective-permute-start | bytes 98312 | tf_op jit(solution)/shard_map/ppermute | solution.py:18
  11.0 5.8 %collective-permute-start.3 = (f32[2,16,1,256]{3,2,1,0:T(1,128)S(1)}, f32[2,16,1,256]{3,2,1,0:T(1,128)S(1)}, u32[]{:S(2)}, u32[]{:S(2)}) collective-permute-start(f32[2,16,1,256]{3,2,1,0:T(1,128)S(1)} %get-tuple-element.283), channel_id=1, source_target_pairs={{1,0},{2,1},{3,2},{5,4},{6,5},{7,6},{9,8},{10,9},{11,10},{13,12},{... | collective-permute-start | bytes 98312 | tf_op jit(solution)/shard_map/ppermute | solution.py:20
  13.8 0.7 %copy-start.2 = (f32[16,8,256]{2,1,0:T(8,128)}, f32[16,8,256]{2,1,0:T(8,128)S(1)}, u32[]{:S(2)}) copy-start(f32[16,8,256]{2,1,0:T(8,128)S(1)} %broadcast_add_fusion) | copy-start | bytes 393220
  17.3 0.9 %slice-start = ((f32[16,8,256]{2,1,0:T(8,128)}), f32[14,8,256]{2,1,0:T(8,128)S(1)}, s32[]{:S(2)}) async-start(f32[16,8,256]{2,1,0:T(8,128)} %copy-done.2), calls=%async_computation | async-start | bytes 229376 | tf_op jit(solution)/shard_map/slice | solution.py:64
  19.1 0.9 %copy-start.3 = (f32[16,8,256]{2,1,0:T(8,128)S(1)}, f32[16,8,256]{2,1,0:T(8,128)}, u32[]{:S(2)}) copy-start(f32[16,8,256]{2,1,0:T(8,128)} %copy-done.2) | copy-start | bytes 393220
  20.1 5.3 %collective-permute-start.4 = (f32[4,2,8,256]{3,2,1,0:T(8,128)S(1)}, f32[4,2,8,256]{3,2,1,0:T(8,128)S(1)}, u32[]{:S(2)}, u32[]{:S(2)}) collective-permute-start(f32[4,2,8,256]{3,2,1,0:T(8,128)S(1)} %get-tuple-element.313), channel_id=1, source_target_pairs={{0,4},{4,8},{8,12},{12,16},{16,20},{20,24},{24,28},{28,0},{1,5},{5... | collective-permute-start | bytes 196616 | tf_op jit(solution)/shard_map/ppermute | solution.py:171
  20.2 5.2 %collective-permute-start.5 = (f32[4,2,8,256]{3,2,1,0:T(8,128)S(1)}, f32[4,2,8,256]{3,2,1,0:T(8,128)S(1)}, u32[]{:S(2)}, u32[]{:S(2)}) collective-permute-start(f32[4,2,8,256]{3,2,1,0:T(8,128)S(1)} %get-tuple-element.313), channel_id=1, source_target_pairs={{0,28},{4,0},{8,4},{12,8},{16,12},{20,16},{24,20},{28,24},{1,29},{... | collective-permute-start | bytes 196616 | tf_op jit(solution)/shard_map/ppermute | solution.py:176
  25.4 4.6 %collective-permute-start.6 = (f32[4,2,8,256]{3,2,1,0:T(8,128)S(1)}, f32[4,2,8,256]{3,2,1,0:T(8,128)S(1)}, u32[]{:S(2)}, u32[]{:S(2)}) collective-permute-start(f32[4,2,8,256]{3,2,1,0:T(8,128)S(1)} %collective-permute-done.4), channel_id=1, source_target_pairs={{0,4},{4,8},{8,12},{12,16},{16,20},{20,24},{24,28},{28,0},{1,5},{5... | collective-permute-start | bytes 196616 | tf_op jit(solution)/shard_map/ppermute | solution.py:171
  25.4 4.7 %collective-permute-start.7 = (f32[4,2,8,256]{3,2,1,0:T(8,128)S(1)}, f32[4,2,8,256]{3,2,1,0:T(8,128)S(1)}, u32[]{:S(2)}, u32[]{:S(2)}) collective-permute-start(f32[4,2,8,256]{3,2,1,0:T(8,128)S(1)} %collective-permute-done.5), channel_id=1, source_target_pairs={{0,28},{4,0},{8,4},{12,8},{16,12},{20,16},{24,20},{28,24},{1,29},{... | collective-permute-start | bytes 196616 | tf_op jit(solution)/shard_map/ppermute | solution.py:176
  30.0 4.6 %collective-permute-start.8 = (f32[4,2,8,256]{3,2,1,0:T(8,128)S(1)}, f32[4,2,8,256]{3,2,1,0:T(8,128)S(1)}, u32[]{:S(2)}, u32[]{:S(2)}) collective-permute-start(f32[4,2,8,256]{3,2,1,0:T(8,128)S(1)} %collective-permute-done.6), channel_id=1, source_target_pairs={{0,4},{4,8},{8,12},{12,16},{16,20},{20,24},{24,28},{28,0},{1,5},{5... | collective-permute-start | bytes 196616 | tf_op jit(solution)/shard_map/ppermute | solution.py:171
  30.1 4.7 %collective-permute-start.9 = (f32[4,2,8,256]{3,2,1,0:T(8,128)S(1)}, f32[4,2,8,256]{3,2,1,0:T(8,128)S(1)}, u32[]{:S(2)}, u32[]{:S(2)}) collective-permute-start(f32[4,2,8,256]{3,2,1,0:T(8,128)S(1)} %collective-permute-done.7), channel_id=1, source_target_pairs={{0,28},{4,0},{8,4},{12,8},{16,12},{20,16},{24,20},{28,24},{1,29},{... | collective-permute-start | bytes 196616 | tf_op jit(solution)/shard_map/ppermute | solution.py:176
  34.6 4.6 %collective-permute-start.10 = (f32[4,2,8,256]{3,2,1,0:T(8,128)S(1)}, f32[4,2,8,256]{3,2,1,0:T(8,128)S(1)}, u32[]{:S(2)}, u32[]{:S(2)}) collective-permute-start(f32[4,2,8,256]{3,2,1,0:T(8,128)S(1)} %collective-permute-done.8), channel_id=1, source_target_pairs={{0,4},{4,8},{8,12},{12,16},{16,20},{20,24},{24,28},{28,0},{1,5},{5... | collective-permute-start | bytes 196616 | tf_op jit(solution)/shard_map/ppermute | solution.py:171
